TPU v7x, 32 devices: a whole 2x2x4 slice. The times are simulated.
32 devices in a mesh: slab: 2 (over y), tile: 4 (over z), view: 4 (over x, core).
Axes of the slice: x: 2, y: 2, z: 4, core: 2. Of those that a mesh axis runs over, the one named last changes fastest.
Arguments:
- recorded: float32 [4, 96, 32, 1024], P('view', 'tile', 'slab'), parts along dimension 2, may hold values from 0.5 to 2
- psf_taps: float32 [4, 3, 15], P('view'), may hold values from 0.2 to 1
- estimate: float32 [96, 32, 1024], P('tile', 'slab'), parts along dimension 1, may hold values from 0.5 to 2
Outputs:
- joined: float32 [96, 32, 1024], P('tile', 'slab'), parts along dimension 1
There are 2 independent parts, one for each index of `slab`. A program takes and returns all parts, laid end to end along the dimension named above; an argument that names none is the same for every part. Nothing has to cross between parts.
All inputs are finite; a program needn't handle non-finite values.
Results may differ from a plain program's by a relative error of at most 0.00002.
Values sent between devices are 32-bit elements; how exact they have to be, the bound alone decides.
A program may use at most 64 MiB of HBM per device.

v0:
```python
import jax
import jax.numpy as jnp
from jax import lax
from jax.sharding import PartitionSpec as P

RADIUS = 7
ITERS = 2


def with_halo(shard, sides, width):
    for axis, dim in sides:
        devices, length = (lax.axis_size(axis), shard.shape[dim])
        up = [(i, (i + 1) % devices) for i in range(devices - 1)]
        down = [(j, i) for i, j in up]
        last = lax.slice_in_dim(shard, length - width, length, axis=dim)
        initial = lax.slice_in_dim(shard, 0, width, axis=dim)
        before = lax.ppermute(last, axis, up)
        after = lax.ppermute(initial, axis, down)
        shard = jnp.concatenate([before, shard, after], axis=dim)
    return shard


def valid_along(padded, kernel_row, axis_num, mirrored):
    length_out = padded.shape[axis_num] - 2 * RADIUS
    summed = jnp.zeros(
        padded.shape[:axis_num] + (length_out,) + padded.shape[axis_num + 1 :], jnp.float32
    )
    for offset in range(2 * RADIUS + 1):
        weight = kernel_row[2 * RADIUS - offset] if mirrored else kernel_row[offset]
        summed = summed + weight * lax.slice_in_dim(
            padded, offset, offset + length_out, axis=axis_num
        )
    return summed


def along(values_in, kernel_row, axis_num, mirrored):
    widths = [(0, 0)] * values_in.ndim
    widths[axis_num] = (RADIUS, RADIUS)
    return valid_along(jnp.pad(values_in, widths), kernel_row, axis_num, mirrored)


def finish_zy(values_in, kernel_view, mirrored):
    result = along(values_in, kernel_view[1], 1, mirrored)
    return along(result, kernel_view[2], 2, mirrored)


def local(recorded, psf_taps, estimate):
    kernel = psf_taps / jnp.sum(psf_taps, axis=2, keepdims=True)
    local_views = recorded.shape[0]
    view_total = lax.axis_size("view") * local_views
    for iteration in range(ITERS):
        extended = with_halo(estimate, (("tile", 0),), RADIUS)
        kernel_view = kernel[0]
        blurred = finish_zy(valid_along(extended, kernel_view[0], 0, False), kernel_view, False)
        quotient = recorded[0] / blurred
        quotient_wide = with_halo(quotient, (("tile", 0),), RADIUS)
        correction = finish_zy(
            valid_along(quotient_wide, kernel_view[0], 0, True), kernel_view, True
        )
        log_terms = jnp.log(correction)
        log_total = lax.psum(log_terms, "view")
        estimate = estimate * jnp.exp(log_total / view_total)
    return estimate


def solution(mesh):
    in_specs = (P("view", "tile", "slab", None), P("view", None, None), P("tile", "slab", None))
    out_specs = P("tile", "slab", None)
    return jax.shard_map(local, mesh=mesh, in_specs=in_specs, out_specs=out_specs, check_vma=False)
```

profile of v0, /device:TPU:0, one launch (start us, length us, event | category | flops | bytes accessed | tf_op | source)
XLA Modules:
  0.0 333.8 jit_solution(3361568924771776846)
XLA Ops:
  6.5 1.3 fusion.365
  7.9 5.0 %collective-permute-start = (f32[7,16,1024]{2,1,0:T(8,128)S(1)}, f32[7,16,1024]{2,1,0:T(8,128)S(1)}, u32[]{:S(2)}, u32[]{:S(2)}) collective-permute-start(f32[7,16,1024]{2,1,0:T(8,128)S(1)} %get-tuple-element.13), channel_id=1, source_target_pairs={{0,4},{4,8},{8,12},{1,5},{5,9},{9,13},{2,6},{6,10},{10,14},{3,7},{... | collective-permute-start | bytes 1376264 | tf_op jit(solution)/shard_map/ppermute | solution.py:17
  12.9 1.3 collective-permute-start.1
  14.2 0.1 reduce_sum.9
  14.3 0.1 broadcast_divide_fusion
  14.4 0.7 fusion.367
  15.1 0.6 fusion.368
  15.7 0.7 fusion.366
  16.5 6.1 %collective-permute-done = f32[7,16,1024]{2,1,0:T(8,128)S(1)} collective-permute-done((f32[7,16,1024]{2,1,0:T(8,128)S(1)}, f32[7,16,1024]{2,1,0:T(8,128)S(1)}, u32[]{:S(2)}, u32[]{:S(2)}) %collective-permute-start) | collective-permute-done | bytes 458784 | tf_op jit(solution)/shard_map/ppermute | solution.py:17
  22.6 0.4 constant_dynamic-update-slice_fusion
  23.0 3.7 %collective-permute-done.1 = f32[7,16,1024]{2,1,0:T(8,128)S(1)} collective-permute-done((f32[7,16,1024]{2,1,0:T(8,128)S(1)}, f32[7,16,1024]{2,1,0:T(8,128)S(1)}, u32[]{:S(2)}, u32[]{:S(2)}) %collective-permute-start.1) | collective-permute-done | bytes 458784 | tf_op jit(solution)/shard_map/ppermute | solution.py:18
  26.8 12.1 %fusion.346 = f32[24,16,1024]{2,1,0:T(8,128)S(1)} fusion(f32[31,16,1024]{2,1,0:T(8,128)S(1)} %constant_dynamic-update-slice_fusion.2, f32[31,16,1024]{2,1,0:T(8,128)S(1)} %get-tuple-element.11, f32[24,16,1024]{2,1,0:T(8,128)S(1)} %copy-done, f32[]{:T(128)} %bitcast.19, f32[]{:T(128)} %bitcast.18, f32[]{:T(128)} %bitcast.17, f32[]{:T(128)} %bitcast.16, ...), kind=kLoop, calls=%fused_computation.537 | loop fusion | flops 11403264 | bytes 25165884 | tf_op jit(solution)/shard_map/add | solution.py:30
  38.8 0.0 copy-start.1
  38.8 12.4 %fusion.242 = f32[24,16,1024]{2,1,0:T(8,128)S(1)} fusion(f32[24,16,1024]{2,1,0:T(8,128)S(1)} %fusion.346, f32[]{:T(128)} %bitcast.32, f32[]{:T(128)} %bitcast.31, f32[]{:T(128)} %bitcast.30, f32[]{:T(128)} %bitcast.29, f32[]{:T(128)} %bitcast.28, f32[]{:T(128)} %bitcast.27, f32[]{:T(128)} %bitcast.26, f32[]{:T(128)} %bitcast.25, f32[]{:T(128)} %bitcast.24, ...), kind=kLoop, calls=%fused_computation.426 | loop fusion | flops 11403264 | bytes 3145788 | tf_op jit(solution)/shard_map/add | solution.py:30
  51.2 15.3 %fusion.15 = f32[24,16,1024]{2,1,0:T(8,128)S(1)} fusion(f32[24,16,1024]{2,1,0:T(8,128)S(1)} %fusion.242, f32[1,24,16,1024]{3,2,1,0:T(8,128)S(1)} %copy-done.1, f32[]{:T(128)} %bitcast.45, f32[]{:T(128)} %bitcast.44, f32[]{:T(128)} %bitcast.43, f32[]{:T(128)} %bitcast.42, f32[]{:T(128)} %bitcast.41, f32[]{:T(128)} %bitcast.40, f32[]{:T(128)} %bitcast.39, ...), kind=kLoop, calls=%fused_computation.199 | loop fusion | flops 11796480 | bytes 4718652 | tf_op jit(solution)/shard_map/div | solution.py:55
  66.6 0.1 fusion.364
  66.6 1.3 collective-permute-start.3
  67.9 4.8 %collective-permute-start.2 = (f32[7,16,1024]{2,1,0:T(8,128)S(1)}, f32[7,16,1024]{2,1,0:T(8,128)S(1)}, u32[]{:S(2)}, u32[]{:S(2)}) collective-permute-start(f32[7,16,1024]{2,1,0:T(8,128)S(1)} %get-tuple-element.9), channel_id=1, source_target_pairs={{0,4},{4,8},{8,12},{1,5},{5,9},{9,13},{2,6},{6,10},{10,14},{3,7},{... | collective-permute-start | bytes 1376264 | tf_op jit(solution)/shard_map/ppermute | solution.py:17
  72.7 6.9 %collective-permute-done.3 = f32[7,16,1024]{2,1,0:T(8,128)S(1)} collective-permute-done((f32[7,16,1024]{2,1,0:T(8,128)S(1)}, f32[7,16,1024]{2,1,0:T(8,128)S(1)}, u32[]{:S(2)}, u32[]{:S(2)}) %collective-permute-start.3) | collective-permute-done | bytes 458784 | tf_op jit(solution)/shard_map/ppermute | solution.py:18
  79.6 1.2 collective-permute-done.2
  80.8 12.3 %fusion.193 = f32[24,16,1024]{2,1,0:T(8,128)S(1)} fusion(f32[24,16,1024]{2,1,0:T(8,128)S(1)} %fusion.15, f32[7,16,1024]{2,1,0:T(8,128)S(1)} %collective-permute-done.3, f32[7,16,1024]{2,1,0:T(8,128)S(1)} %collective-permute-done.2, f32[]{:T(128)} %bitcast.19, f32[]{:T(128)} %bitcast.18, f32[]{:T(128)} %bitcast.17, f32[]{:T(128)} %bitcast.16, f32[]{:T(128)} %bitcast.15, ...), kind=kLoop, calls=%fused_computation.377 | loop fusion | flops 16908288 | bytes 4063292 | tf_op jit(solution)/shard_map/add | solution.py:30
  93.0 12.2 %fusion.270 = f32[24,16,1024]{2,1,0:T(8,128)S(1)} fusion(f32[24,16,1024]{2,1,0:T(8,128)S(1)} %fusion.193, f32[]{:T(128)} %bitcast.32, f32[]{:T(128)} %bitcast.31, f32[]{:T(128)} %bitcast.30, f32[]{:T(128)} %bitcast.29, f32[]{:T(128)} %bitcast.28, f32[]{:T(128)} %bitcast.27, f32[]{:T(128)} %bitcast.26, f32[]{:T(128)} %bitcast.25, f32[]{:T(128)} %bitcast.24, ...), kind=kLoop, calls=%fused_computation.454 | loop fusion | flops 11403264 | bytes 3145788 | tf_op jit(solution)/shard_map/add | solution.py:30
  105.3 16.2 %fusion.361 = f32[24,16,1024]{2,1,0:T(8,128)} fusion(f32[24,16,1024]{2,1,0:T(8,128)S(1)} %fusion.270, f32[]{:T(128)} %bitcast.45, f32[]{:T(128)} %bitcast.44, f32[]{:T(128)} %bitcast.43, f32[]{:T(128)} %bitcast.42, f32[]{:T(128)} %bitcast.41, f32[]{:T(128)} %bitcast.40, f32[]{:T(128)} %bitcast.39, f32[]{:T(128)} %bitcast.38, f32[]{:T(128)} %bitcast.37, ...), kind=kLoop, calls=%fused_computation.567 | loop fusion | flops 11403264 | bytes 3145788 | tf_op jit(solution)/shard_map/log | solution.py:60
  121.5 0.0 all-reduce.11.cloned.1.call-update
  121.5 0.0 all-reduce.13.cloned.1.call-start
  121.6 45.1 %all-reduce.11.cloned.1.call-done = f32[24,16,1024]{2,1,0:T(8,128)} async-done(((f32[24,16,1024]{2,1,0:T(8,128)}), f32[24,16,1024]{2,1,0:T(8,128)}) %all-reduce.11.cloned.1.call-update) | async-done | bytes 1572880 | tf_op jit(solution)/shard_map/psum | solution.py:61
  166.7 1.7 exponential_multiply_fusion.1
  168.4 0.1 fusion.363
  168.5 1.3 collective-permute-start.5
  169.8 4.6 %collective-permute-start.4 = (f32[7,16,1024]{2,1,0:T(8,128)S(1)}, f32[7,16,1024]{2,1,0:T(8,128)S(1)}, u32[]{:S(2)}, u32[]{:S(2)}) collective-permute-start(f32[7,16,1024]{2,1,0:T(8,128)S(1)} %get-tuple-element.7), channel_id=1, source_target_pairs={{0,4},{4,8},{8,12},{1,5},{5,9},{9,13},{2,6},{6,10},{10,14},{3,7},{... | collective-permute-start | bytes 1376264 | tf_op jit(solution)/shard_map/ppermute | solution.py:17
  174.3 8.1 %collective-permute-done.5 = f32[7,16,1024]{2,1,0:T(8,128)S(1)} collective-permute-done((f32[7,16,1024]{2,1,0:T(8,128)S(1)}, f32[7,16,1024]{2,1,0:T(8,128)S(1)}, u32[]{:S(2)}, u32[]{:S(2)}) %collective-permute-start.5) | collective-permute-done | bytes 458784 | tf_op jit(solution)/shard_map/ppermute | solution.py:18
  182.5 1.2 collective-permute-done.4
  183.7 12.2 %fusion.155 = f32[24,16,1024]{2,1,0:T(8,128)S(1)} fusion(f32[24,16,1024]{2,1,0:T(8,128)S(1)} %exponential_multiply_fusion.1, f32[7,16,1024]{2,1,0:T(8,128)S(1)} %collective-permute-done.5, f32[7,16,1024]{2,1,0:T(8,128)S(1)} %collective-permute-done.4, f32[]{:T(128)} %bitcast.19, f32[]{:T(128)} %bitcast.18, f32[]{:T(128)} %bitcast.17, f32[]{:T(128)} %bitcast.16, ...), kind=kLoop, calls=%fused_computation.339 | loop fusion | flops 16908288 | bytes 4063292 | tf_op jit(solution)/shard_map/add | solution.py:30
  195.8 0.0 copy-start.2
  195.8 12.4 %fusion.298 = f32[24,16,1024]{2,1,0:T(8,128)S(1)} fusion(f32[24,16,1024]{2,1,0:T(8,128)S(1)} %fusion.155, f32[]{:T(128)} %bitcast.32, f32[]{:T(128)} %bitcast.31, f32[]{:T(128)} %bitcast.30, f32[]{:T(128)} %bitcast.29, f32[]{:T(128)} %bitcast.28, f32[]{:T(128)} %bitcast.27, f32[]{:T(128)} %bitcast.26, f32[]{:T(128)} %bitcast.25, f32[]{:T(128)} %bitcast.24, ...), kind=kLoop, calls=%fused_computation.482 | loop fusion | flops 11403264 | bytes 3145788 | tf_op jit(solution)/shard_map/add | solution.py:30
  208.2 0.0 copy-done.2
  208.2 15.3 %fusion.72 = f32[24,16,1024]{2,1,0:T(8,128)S(1)} fusion(f32[24,16,1024]{2,1,0:T(8,128)S(1)} %fusion.298, f32[1,24,16,1024]{3,2,1,0:T(8,128)S(1)} %copy-done.2, f32[]{:T(128)} %bitcast.45, f32[]{:T(128)} %bitcast.44, f32[]{:T(128)} %bitcast.43, f32[]{:T(128)} %bitcast.42, f32[]{:T(128)} %bitcast.41, f32[]{:T(128)} %bitcast.40, f32[]{:T(128)} %bitcast.39, ...), kind=kLoop, calls=%fused_computation.256 | loop fusion | flops 11796480 | bytes 4718652 | tf_op jit(solution)/shard_map/div | solution.py:55
  223.5 0.1 fusion.362
  223.6 1.5 collective-permute-start.7
  225.2 5.0 %collective-permute-start.6 = (f32[7,16,1024]{2,1,0:T(8,128)S(1)}, f32[7,16,1024]{2,1,0:T(8,128)S(1)}, u32[]{:S(2)}, u32[]{:S(2)}) collective-permute-start(f32[7,16,1024]{2,1,0:T(8,128)S(1)} %get-tuple-element.5), channel_id=1, source_target_pairs={{0,4},{4,8},{8,12},{1,5},{5,9},{9,13},{2,6},{6,10},{10,14},{3,7},{... | collective-permute-start | bytes 1376264 | tf_op jit(solution)/shard_map/ppermute | solution.py:17
  230.2 7.0 %collective-permute-done.7 = f32[7,16,1024]{2,1,0:T(8,128)S(1)} collective-permute-done((f32[7,16,1024]{2,1,0:T(8,128)S(1)}, f32[7,16,1024]{2,1,0:T(8,128)S(1)}, u32[]{:S(2)}, u32[]{:S(2)}) %collective-permute-start.7) | collective-permute-done | bytes 458784 | tf_op jit(solution)/shard_map/ppermute | solution.py:18
  237.2 1.4 collective-permute-done.6
  238.6 12.2 %fusion.117 = f32[24,16,1024]{2,1,0:T(8,128)S(1)} fusion(f32[24,16,1024]{2,1,0:T(8,128)S(1)} %fusion.72, f32[7,16,1024]{2,1,0:T(8,128)S(1)} %collective-permute-done.7, f32[7,16,1024]{2,1,0:T(8,128)S(1)} %collective-permute-done.6, f32[]{:T(128)} %bitcast.19, f32[]{:T(128)} %bitcast.18, f32[]{:T(128)} %bitcast.17, f32[]{:T(128)} %bitcast.16, f32[]{:T(128)} %bitcast.15, ...), kind=kLoop, calls=%fused_computation.301 | loop fusion | flops 16908288 | bytes 4063292 | tf_op jit(solution)/shard_map/add | solution.py:30
  250.8 12.2 %fusion.326 = f32[24,16,1024]{2,1,0:T(8,128)S(1)} fusion(f32[24,16,1024]{2,1,0:T(8,128)S(1)} %fusion.117, f32[]{:T(128)} %bitcast.32, f32[]{:T(128)} %bitcast.31, f32[]{:T(128)} %bitcast.30, f32[]{:T(128)} %bitcast.29, f32[]{:T(128)} %bitcast.28, f32[]{:T(128)} %bitcast.27, f32[]{:T(128)} %bitcast.26, f32[]{:T(128)} %bitcast.25, f32[]{:T(128)} %bitcast.24, ...), kind=kLoop, calls=%fused_computation.510 | loop fusion | flops 11403264 | bytes 3145788 | tf_op jit(solution)/shard_map/add | solution.py:30
  263.0 16.2 %fusion.360 = f32[24,16,1024]{2,1,0:T(8,128)} fusion(f32[24,16,1024]{2,1,0:T(8,128)S(1)} %fusion.326, f32[]{:T(128)} %bitcast.45, f32[]{:T(128)} %bitcast.44, f32[]{:T(128)} %bitcast.43, f32[]{:T(128)} %bitcast.42, f32[]{:T(128)} %bitcast.41, f32[]{:T(128)} %bitcast.40, f32[]{:T(128)} %bitcast.39, f32[]{:T(128)} %bitcast.38, f32[]{:T(128)} %bitcast.37, ...), kind=kLoop, calls=%fused_computation.566 | loop fusion | flops 11403264 | bytes 3145788 | tf_op jit(solution)/shard_map/log | solution.py:60
  279.2 0.0 all-reduce.13.cloned.1.call-update
  279.2 44.9 %all-reduce.13.cloned.1.call-done = f32[24,16,1024]{2,1,0:T(8,128)} async-done(((f32[24,16,1024]{2,1,0:T(8,128)}), f32[24,16,1024]{2,1,0:T(8,128)}) %all-reduce.13.cloned.1.call-update) | async-done | bytes 1572880 | tf_op jit(solution)/shard_map/psum | solution.py:61
  324.1 2.8 exponential_multiply_fusion
  (8 shorter events, 0.1 us)
Async XLA Ops:
  6.5 16.1 %copy-start = (f32[24,16,1024]{2,1,0:T(8,128)S(1)}, f32[24,16,1024]{2,1,0:T(8,128)}, u32[]{:S(2)}) copy-start(f32[24,16,1024]{2,1,0:T(8,128)} %param.5) | copy-start | bytes 4718596
  6.5 7.6 %copy-start.3 = (f32[1,3,15]{2,0,1:T(1,128)S(1)}, f32[1,3,15]{2,0,1:T(1,128)}, u32[]{:S(2)}) copy-start(f32[1,3,15]{2,0,1:T(1,128)} %param.4) | copy-start | bytes 544
  6.5 160.1 %all-reduce.11.cloned.1.call-start = ((), (), s32[]{:S(2)}) async-start(), calls=%async_computation | async-start | bytes 3145728 | tf_op jit(solution)/shard_map/psum | solution.py:61
  7.9 14.7 %collective-permute-start = (f32[7,16,1024]{2,1,0:T(8,128)S(1)}, f32[7,16,1024]{2,1,0:T(8,128)S(1)}, u32[]{:S(2)}, u32[]{:S(2)}) collective-permute-start(f32[7,16,1024]{2,1,0:T(8,128)S(1)} %get-tuple-element.13), channel_id=1, source_target_pairs={{0,4},{4,8},{8,12},{1,5},{5,9},{9,13},{2,6},{6,10},{10,14},{3,7},{... | collective-permute-start | bytes 1376264 | tf_op jit(solution)/shard_map/ppermute | solution.py:17
  12.9 13.9 %collective-permute-start.1 = (f32[7,16,1024]{2,1,0:T(8,128)S(1)}, f32[7,16,1024]{2,1,0:T(8,128)S(1)}, u32[]{:S(2)}, u32[]{:S(2)}) collective-permute-start(f32[7,16,1024]{2,1,0:T(8,128)S(1)} %get-tuple-element.14), channel_id=1, source_target_pairs={{4,0},{8,4},{12,8},{5,1},{9,5},{13,9},{6,2},{10,6},{14,10},{7,3},{... | collective-permute-start | bytes 1376264 | tf_op jit(solution)/shard_map/ppermute | solution.py:18
  38.8 12.4 %copy-start.1 = (f32[1,24,16,1024]{3,2,1,0:T(8,128)S(1)}, f32[1,24,16,1024]{3,2,1,0:T(8,128)}, u32[]{:S(2)}) copy-start(f32[1,24,16,1024]{3,2,1,0:T(8,128)} %param.3) | copy-start | bytes 4718596
  66.6 13.0 %collective-permute-start.3 = (f32[7,16,1024]{2,1,0:T(8,128)S(1)}, f32[7,16,1024]{2,1,0:T(8,128)S(1)}, u32[]{:S(2)}, u32[]{:S(2)}) collective-permute-start(f32[7,16,1024]{2,1,0:T(8,128)S(1)} %get-tuple-element.10), channel_id=1, source_target_pairs={{4,0},{8,4},{12,8},{5,1},{9,5},{13,9},{6,2},{10,6},{14,10},{7,3},{... | collective-permute-start | bytes 1376264 | tf_op jit(solution)/shard_map/ppermute | solution.py:18
  67.9 12.8 %collective-permute-start.2 = (f32[7,16,1024]{2,1,0:T(8,128)S(1)}, f32[7,16,1024]{2,1,0:T(8,128)S(1)}, u32[]{:S(2)}, u32[]{:S(2)}) collective-permute-start(f32[7,16,1024]{2,1,0:T(8,128)S(1)} %get-tuple-element.9), channel_id=1, source_target_pairs={{0,4},{4,8},{8,12},{1,5},{5,9},{9,13},{2,6},{6,10},{10,14},{3,7},{... | collective-permute-start | bytes 1376264 | tf_op jit(solution)/shard_map/ppermute | solution.py:17
  121.5 202.6 %all-reduce.13.cloned.1.call-start = ((), (), s32[]{:S(2)}) async-start(), calls=%async_computation.1 | async-start | bytes 3145728 | tf_op jit(solution)/shard_map/psum | solution.py:61
  168.5 14.0 %collective-permute-start.5 = (f32[7,16,1024]{2,1,0:T(8,128)S(1)}, f32[7,16,1024]{2,1,0:T(8,128)S(1)}, u32[]{:S(2)}, u32[]{:S(2)}) collective-permute-start(f32[7,16,1024]{2,1,0:T(8,128)S(1)} %get-tuple-element.8), channel_id=1, source_target_pairs={{4,0},{8,4},{12,8},{5,1},{9,5},{13,9},{6,2},{10,6},{14,10},{7,3},{... | collective-permute-start | bytes 1376264 | tf_op jit(solution)/shard_map/ppermute | solution.py:18
  169.8 13.9 %collective-permute-start.4 = (f32[7,16,1024]{2,1,0:T(8,128)S(1)}, f32[7,16,1024]{2,1,0:T(8,128)S(1)}, u32[]{:S(2)}, u32[]{:S(2)}) collective-permute-start(f32[7,16,1024]{2,1,0:T(8,128)S(1)} %get-tuple-element.7), channel_id=1, source_target_pairs={{0,4},{4,8},{8,12},{1,5},{5,9},{9,13},{2,6},{6,10},{10,14},{3,7},{... | collective-permute-start | bytes 1376264 | tf_op jit(solution)/shard_map/ppermute | solution.py:17
  195.8 12.4 %copy-start.2 = (f32[1,24,16,1024]{3,2,1,0:T(8,128)S(1)}, f32[1,24,16,1024]{3,2,1,0:T(8,128)}, u32[]{:S(2)}) copy-start(f32[1,24,16,1024]{3,2,1,0:T(8,128)} %param.3) | copy-start | bytes 4718596
  223.6 13.6 %collective-permute-start.7 = (f32[7,16,1024]{2,1,0:T(8,128)S(1)}, f32[7,16,1024]{2,1,0:T(8,128)S(1)}, u32[]{:S(2)}, u32[]{:S(2)}) collective-permute-start(f32[7,16,1024]{2,1,0:T(8,128)S(1)} %get-tuple-element.6), channel_id=1, source_target_pairs={{4,0},{8,4},{12,8},{5,1},{9,5},{13,9},{6,2},{10,6},{14,10},{7,3},{... | collective-permute-start | bytes 1376264 | tf_op jit(solution)/shard_map/ppermute | solution.py:18
  225.2 13.4 %collective-permute-start.6 = (f32[7,16,1024]{2,1,0:T(8,128)S(1)}, f32[7,16,1024]{2,1,0:T(8,128)S(1)}, u32[]{:S(2)}, u32[]{:S(2)}) collective-permute-start(f32[7,16,1024]{2,1,0:T(8,128)S(1)} %get-tuple-element.5), channel_id=1, source_target_pairs={{0,4},{4,8},{8,12},{1,5},{5,9},{9,13},{2,6},{6,10},{10,14},{3,7},{... | collective-permute-start | bytes 1376264 | tf_op jit(solution)/shard_map/ppermute | solution.py:17
Sparse Core Ops, SparseCore 0:
  121.6 44.9 all-reduce.10
  279.3 44.7 all-reduce.12
where the time goes:
time: 336 us; the launch traced here: 334 us
  other arithmetic  166 us (49%)
  waiting for transfers between devices  126 us (38%)
  starting transfers between devices  24.8 us (7%)
  between operations  13.7 us (4%)
  local copies, waits for them, and re-layouts  4.11 us (1%)
    add x8, other arithmetic, valid_along(): summed + weight * lax.slice_in_dim(padded, offset, offset + length_out, a...  97.8 us
    psum x2, waiting for transfers between devices, local(): log_total = lax.psum(log_terms, 'view')  90 us
    log x2, other arithmetic, local(): log_terms = jnp.log(correction)  32.4 us
    div x2, other arithmetic, local(): quotient = recorded[0] / blurred  30.7 us
    ppermute x4, waiting for transfers between devices, with_halo(): after = lax.ppermute(initial, axis, down)  25.7 us
    ppermute x4, starting transfers between devices, with_halo(): before = lax.ppermute(last, axis, up)  19.3 us
    ppermute x4, waiting for transfers between devices, with_halo(): before = lax.ppermute(last, axis, up)  9.9 us
  transfers between devices with their start and end apart: 10, of which 10 were waited for; matrix products, arithmetic and copies ran while one was open for 1% of the time, Pallas kernels for 0%

commit v1 on v0

v1 whole, which is shorter than its diff:
```python
import functools

import jax
import jax.numpy as jnp
from jax import lax
from jax.experimental import pallas as pl
from jax.experimental.pallas import tpu as pltpu
from jax.sharding import PartitionSpec as P

RADIUS = 7
TAPS = 2 * RADIUS + 1
ITERS = 2
LANE = 128
CORES = 2
F32 = jnp.float32
BF16 = jnp.bfloat16
MESH = pl.DeviceIdType.MESH


def split(value):
    hi = value.astype(BF16)
    return hi, (value - hi.astype(F32)).astype(BF16)


def dot(a, b):
    return jnp.dot(a, b, preferred_element_type=F32)


def pieces(total, size):
    return [(start, min(size, total - start)) for start in range(0, total, size)]


def window_of(chip, chips, ny):
    part = ny // chips
    width = part + LANE * min(chips - 1, 2)
    start = jnp.clip(chip * part - LANE, 0, ny - width)
    return pl.multiple_of(start, LANE), width


def body(
    nx, nz, ny, tiles, views,
    rec_ref, taps_ref, est_ref, out_ref,
    est_x, quo_x, rec_in, acc, acc_in, kern, mat_xz, mat_y, u_hi, u_lo,
    kern_send, kern_recv, rec_send, rec_recv, rim_send, rim_recv,
    acc_send, acc_recv, out_send, out_recv, fwd_send, fwd_recv,
):
    chips = views // CORES
    part = ny // chips
    rows = nx * nz
    rim = RADIUS * nz
    half = rows // 2
    tile = lax.axis_index("tile")
    view = lax.axis_index("view")
    chip, core = view // CORES, view % CORES
    mate = chip * CORES + (1 - core)
    start, width = window_of(chip, chips, ny)
    own = slice(rim, rim + rows)

    def chip_at(step):
        return lax.rem(chip + step, chips)

    def peer(step):
        return {"view": chip_at(step) * CORES + core}

    barrier = pltpu.get_barrier_semaphore()
    for step in range(1, chips):
        pl.semaphore_signal(barrier, inc=1, device_id=peer(step), device_id_type=MESH)
    pl.semaphore_signal(barrier, inc=1, device_id={"view": mate}, device_id_type=MESH)

    @pl.when(tile > 0)
    def _():
        pl.semaphore_signal(barrier, inc=1, device_id={"tile": tile - 1}, device_id_type=MESH)

    @pl.when(tile < tiles - 1)
    def _():
        pl.semaphore_signal(barrier, inc=1, device_id={"tile": tile + 1}, device_id_type=MESH)

    taps = taps_ref[...]
    kern[0, 0:3, 0:TAPS] = taps / jnp.sum(taps, axis=1, keepdims=True)
    est_x[own, :] = est_ref[:, pl.ds(start, width)]

    @pl.when(tile == 0)
    def _():
        est_x[0:rim, :] = jnp.zeros((rim, width), F32)
        for s in range(chips):
            quo_x[s, 0:rim, :] = jnp.zeros((rim, width), F32)

    @pl.when(tile == tiles - 1)
    def _():
        est_x[rim + rows :, :] = jnp.zeros((rim, width), F32)
        for s in range(chips):
            quo_x[s, rim + rows :, :] = jnp.zeros((rim, width), F32)

    tile_peers = jnp.minimum(tile, 1) + jnp.minimum(tiles - 1 - tile, 1)
    pl.semaphore_wait(barrier, chips + tile_peers)

    def rim_down(array, number):
        return pltpu.make_async_remote_copy(
            src_ref=array.at[pl.ds(rim, rim)],
            dst_ref=array.at[pl.ds(rim + rows, rim)],
            send_sem=rim_send.at[number, 0],
            recv_sem=rim_recv.at[number, 0],
            device_id={"tile": tile - 1},
            device_id_type=MESH,
        )

    def rim_up(array, number):
        return pltpu.make_async_remote_copy(
            src_ref=array.at[pl.ds(rows, rim)],
            dst_ref=array.at[pl.ds(0, rim)],
            send_sem=rim_send.at[number, 1],
            recv_sem=rim_recv.at[number, 1],
            device_id={"tile": tile + 1},
            device_id_type=MESH,
        )

    def rim_start(array, number, which):
        @pl.when(tile > 0 if which == 0 else tile < tiles - 1)
        def _():
            (rim_up if which else rim_down)(array, number).start()

    def rim_wait(array, number):
        @pl.when(tile > 0)
        def _():
            rim_down(array, number).wait_send()
            rim_up(array, number).wait_recv()

        @pl.when(tile < tiles - 1)
        def _():
            rim_up(array, number).wait_send()
            rim_down(array, number).wait_recv()

    row_parts = [(0, rim, 0), (rows - rim, rim, 1), (rim, rows - 2 * rim, None)]

    rim_start(est_x, 0, 0)
    rim_start(est_x, 0, 1)

    def kern_copy(step):
        return pltpu.make_async_remote_copy(
            src_ref=kern.at[0],
            dst_ref=kern.at[step],
            send_sem=kern_send.at[step],
            recv_sem=kern_recv.at[step],
            device_id=peer(chips - step),
            device_id_type=MESH,
        )

    def rec_copy(step, index):
        row, count, _ = row_parts[index]
        begin, _ = window_of(chip_at(chips - step), chips, ny)
        return pltpu.make_async_remote_copy(
            src_ref=rec_ref.at[pl.ds(row, count), pl.ds(begin, width)],
            dst_ref=rec_in.at[step, pl.ds(row, count)],
            send_sem=rec_send.at[step, index],
            recv_sem=rec_recv.at[step, index],
            device_id=peer(chips - step),
            device_id_type=MESH,
        )

    for step in range(1, chips):
        kern_copy(step).start()
        for index in range(len(row_parts)):
            rec_copy(step, index).start()

    def build(s):
        kern_s = kern[s]
        width_s = mat_xz.shape[-1]
        wide = -(-width_s // LANE) * LANE
        a = lax.broadcasted_iota(jnp.int32, (nz, wide), 0)
        column = lax.broadcasted_iota(jnp.int32, (nz, wide), 1)
        p, b = lax.div(column, jnp.int32(nz)), lax.rem(column, jnp.int32(nz))
        r = lax.broadcasted_iota(jnp.int32, (3 * LANE, LANE), 0)
        c = lax.broadcasted_iota(jnp.int32, (3 * LANE, LANE), 1)
        for mirrored in range(2):
            fx = jnp.zeros((nz, wide), F32)
            fz = jnp.zeros((nz, wide), F32)
            fy = jnp.zeros((3 * LANE, LANE), F32)
            for k in range(TAPS):
                o = TAPS - 1 - k if mirrored else k
                fx = jnp.where(p == k, kern_s[0:1, o : o + 1], fx)
                fz = jnp.where(b - a + RADIUS == k, kern_s[1:2, o : o + 1], fz)
                fy = jnp.where(r - c - LANE + RADIUS == k, kern_s[2:3, o : o + 1], fy)
            strip = fx * fz
            for i in range(nx // 2):
                moved = strip if i == 0 else pltpu.roll(strip, i * nz, 1)
                hi, lo = split(moved)
                mat_xz[s, mirrored, i * nz : (i + 1) * nz, :] = hi[:, :width_s]
                mat_xz[s, mirrored, half + i * nz : half + (i + 1) * nz, :] = lo[:, :width_s]
            for index, value in enumerate(split(fy)):
                mat_y[s, mirrored, index, 0 : 3 * LANE, 0:LANE] = value
                mat_y[s, mirrored, index, LANE : 4 * LANE, LANE : 2 * LANE] = value
                mat_y[s, mirrored, index, 3 * LANE :, 0:LANE] = jnp.zeros((LANE, LANE), BF16)
                mat_y[s, mirrored, index, 0:LANE, LANE : 2 * LANE] = jnp.zeros((LANE, LANE), BF16)

    for u in (u_hi, u_lo):
        u[:, 0:LANE] = jnp.zeros((rows, LANE), BF16)
        u[:, LANE + width :] = jnp.zeros((rows, LANE), BF16)

    def blur(source, s, mirrored, store):
        depth = half + 2 * rim
        for h in range(2):
            for c0, n in pieces(width, 2 * LANE):
                hi, lo = split(source[h * half : h * half + depth, c0 : c0 + n])
                both = dot(mat_xz[s, mirrored], hi)
                value = both[:half] + both[half:] + dot(mat_xz[s, mirrored, :half], lo)
                hi, lo = split(value)
                u_hi[h * half : (h + 1) * half, LANE + c0 : LANE + c0 + n] = hi
                u_lo[h * half : (h + 1) * half, LANE + c0 : LANE + c0 + n] = lo
        for c0, n in pieces(width, 2 * LANE):
            k = n + 2 * LANE
            hi, lo = u_hi[:, c0 : c0 + k], u_lo[:, c0 : c0 + k]
            m_hi, m_lo = mat_y[s, mirrored, 0, :k, :n], mat_y[s, mirrored, 1, :k, :n]
            store(c0, n, dot(hi, m_hi) + dot(lo, m_hi) + dot(hi, m_lo))

    build(0)
    for it in range(ITERS):
        rim_wait(est_x, 0)
        for s in range(chips):
            if it == 0 and s > 0:
                kern_copy(s).wait()
                build(s)
            quo = quo_x.at[s]

            def store_blurred(c0, n, value):
                quo[own, c0 : c0 + n] = value

            blur(est_x, s, 0, store_blurred)
            for index, (row, count, which) in enumerate(row_parts):
                if s == 0:
                    recorded = rec_ref[row : row + count, pl.ds(start, width)]
                else:
                    if it == 0:
                        rec_copy(s, index).wait()
                    recorded = rec_in[s, row : row + count, :]
                here = slice(rim + row, rim + row + count)
                quo[here, :] = recorded / quo[here, :]
                if which is not None:
                    rim_start(quo, 1 + s, which)
        for s in range(chips):
            quo = quo_x.at[s]
            rim_wait(quo, 1 + s)

            def store_log(c0, n, value):
                term = jnp.log(value)
                if s > 0:
                    term = acc[:, c0 : c0 + n] + term
                acc[:, c0 : c0 + n] = term

            blur(quo, s, 1, store_log)
        swap = pltpu.make_async_remote_copy(
            src_ref=acc,
            dst_ref=acc_in.at[it],
            send_sem=acc_send.at[it],
            recv_sem=acc_recv.at[it],
            device_id={"view": mate},
            device_id_type=MESH,
        )
        swap.start()
        swap.wait()
        if it < ITERS - 1:
            est_x[own, :] = est_x[own, :] * jnp.exp((acc[...] + acc_in[it]) / views)
            rim_start(est_x, 0, 0)
            rim_start(est_x, 0, 1)
        else:
            inner = pl.multiple_of(chip * part - start, LANE)
            mine = pl.ds(inner, part)
            there = pl.ds(pl.multiple_of(chip * part, LANE), part)
            out_ref[:, there] = est_x[own, mine] * jnp.exp(
                (acc[:, mine] + acc_in[it, :, mine]) / views
            )

    my_rows = pl.ds(pl.multiple_of(core * half, 8), half)

    def out_copy(step):
        columns = pl.ds(pl.multiple_of(chip * part, LANE), part)
        return pltpu.make_async_remote_copy(
            src_ref=out_ref.at[my_rows, columns],
            dst_ref=out_ref.at[my_rows, columns],
            send_sem=out_send.at[step],
            recv_sem=out_recv.at[step],
            device_id=peer(step),
            device_id_type=MESH,
        )

    def fwd_copy(step):
        columns = pl.ds(pl.multiple_of(chip_at(chips - step) * part, LANE), part)
        return pltpu.make_async_remote_copy(
            src_ref=out_ref.at[my_rows, columns],
            dst_ref=out_ref.at[my_rows, columns],
            send_sem=fwd_send.at[step],
            recv_sem=fwd_recv.at[step],
            device_id={"view": mate},
            device_id_type=MESH,
        )

    for step in range(1, chips):
        out_copy(step).start()
    for step in range(1, chips):
        out_copy(step).wait_recv()
        fwd_copy(step).start()
    for step in range(1, chips):
        out_copy(step).wait_send()
        fwd_copy(step).wait()


def local(tiles, views, recorded, psf_taps, estimate):
    nx, nz, ny = estimate.shape
    rows, rim = nx * nz, RADIUS * nz
    chips = views // CORES
    width = window_of(0, chips, ny)[1]
    vmem = pl.BlockSpec(memory_space=pltpu.VMEM)
    dma = pltpu.SemaphoreType.DMA
    parts = 3
    out = pl.pallas_call(
        functools.partial(body, nx, nz, ny, tiles, views),
        out_shape=jax.ShapeDtypeStruct((rows, ny), F32),
        in_specs=[vmem] * 3,
        out_specs=vmem,
        scratch_shapes=[
            pltpu.VMEM((rows + 2 * rim, width), F32),
            pltpu.VMEM((chips, rows + 2 * rim, width), F32),
            pltpu.VMEM((chips, rows, width), F32),
            pltpu.VMEM((rows, width), F32),
            pltpu.VMEM((ITERS, rows, width), F32),
            pltpu.VMEM((chips, 8, LANE), F32),
            pltpu.VMEM((chips, 2, rows, rows // 2 + 2 * rim), BF16),
            pltpu.VMEM((chips, 2, 2, 4 * LANE, 2 * LANE), BF16),
            pltpu.VMEM((rows, width + 2 * LANE), BF16),
            pltpu.VMEM((rows, width + 2 * LANE), BF16),
            dma((chips,)),
            dma((chips,)),
            dma((chips, parts)),
            dma((chips, parts)),
            dma((1 + chips, 2)),
            dma((1 + chips, 2)),
            dma((ITERS,)),
            dma((ITERS,)),
            dma((chips,)),
            dma((chips,)),
            dma((chips,)),
            dma((chips,)),
        ],
        compiler_params=pltpu.CompilerParams(
            collective_id=0, has_side_effects=True, vmem_limit_bytes=56 * 2**20
        ),
    )(recorded.reshape(rows, ny), psf_taps.reshape(3, TAPS), estimate.reshape(rows, ny))
    return out.reshape(estimate.shape)


def solution(mesh):
    in_specs = (P("view", "tile", "slab", None), P("view", None, None), P("tile", "slab", None))
    out_specs = P("tile", "slab", None)
    sizes = (mesh.shape["tile"], mesh.shape["view"])
    return jax.shard_map(
        functools.partial(local, *sizes),
        mesh=mesh, in_specs=in_specs, out_specs=out_specs, check_vma=False,
    )
```

time: 336 us -> 81.2 us (0.24)
  other arithmetic: 166 us -> 0 us
  waiting for transfers between devices: 126 us -> 0 us
  Pallas kernels: 0 us -> 77.1 us
  starting transfers between devices: 24.8 us -> 0 us
  between operations: 13.7 us -> 0.01 us
    add x8 -> x0, other arithmetic: 97.8 us -> none  [valid_along(): summed + weight * lax.slice_in_dim(padded, offset, offset + length_out, a...]
    psum x2 -> x0, waiting for transfers between devices: 90 us -> none  [local(): log_total = lax.psum(log_terms, 'view')]
    pallas_call x0 -> x1, Pallas kernels: none -> 77.1 us  [local(): pl.pallas_call(functools.partial(body, nx, nz, ny, tiles, views), out_sha...]
    ppermute x8 -> x0, waiting for transfers between devices: 35.6 us -> none  [the longest x4 25.7 us: with_halo(): after = lax.ppermute(initial, axis, down)]
    log x2 -> x0, other arithmetic: 32.4 us -> none  [local(): log_terms = jnp.log(correction)]
    div x3 -> x0, other arithmetic: 30.7 us -> none  [the longest x2 30.7 us: local(): quotient = recorded[0] / blurred]
    ppermute x8 -> x0, starting transfers between devices: 24.7 us -> none  [the longest x4 19.3 us: with_halo(): before = lax.ppermute(last, axis, up)]
    mul x2 -> x0, other arithmetic: 4.55 us -> none  [local(): estimate = estimate * jnp.exp(log_total / view_total)]
  transfers between devices with their start and end apart: 10 -> 0, of which waited for: 10 -> 0; matrix products, arithmetic and copies ran while one was open for 1% -> 0% of each run, Pallas kernels for 0% -> 0%
where the time goes in v1:
time: 81.2 us; the launch traced here: 81 us
  Pallas kernels  77.1 us (95%)
  local copies, waits for them, and re-layouts  3.99 us (5%)
    pallas_call x1, Pallas kernels, local(): pl.pallas_call(functools.partial(body, nx, nz, ny, tiles, views), out_sha...  77.1 us
    unnamed x2, local copies, waits for them, and re-layouts  3.99 us

profile of v1, /device:TPU:0, one launch (start us, length us, event | category | flops | bytes accessed | tf_op | source)
XLA Modules:
  0.0 81.0 jit_solution(14598503243588457861)
XLA Ops:
  0.0 1.3 %copy.6 = f32[1,3,15]{2,1,0:T(4,128)} copy(f32[1,3,15]{2,0,1:T(1,128)} %param.4) | data formatting | bytes 360
  1.3 77.1 %shard_map.37 = f32[384,1024]{1,0:T(8,128)} custom-call(f32[384,1024]{1,0:T(8,128)} %bitcast.7, f32[3,15]{1,0:T(4,128)} %bitcast.9, f32[384,1024]{1,0:T(8,128)} %bitcast.8), custom_call_target="tpu_custom_call" | custom-call | tf_op jit(solution)/shard_map/pallas_call | solution.py:314
  78.3 2.7 %copy.8 = f32[24,16,1024]{2,1,0:T(8,128)} copy(f32[24,16,1024]{2,1,0:T(8,128)} %bitcast.6) | data formatting | bytes 3145728

commit v2 on v1

v2 whole, which is shorter than its diff:
```python
import functools

import jax
import jax.numpy as jnp
from jax import lax
from jax.experimental import pallas as pl
from jax.experimental.pallas import tpu as pltpu
from jax.sharding import PartitionSpec as P

RADIUS = 7
TAPS = 2 * RADIUS + 1
ITERS = 2
LANE = 128
CORES = 2
F32 = jnp.float32
BF16 = jnp.bfloat16
MESH = pl.DeviceIdType.MESH


def split(value):
    hi = value.astype(BF16)
    return hi, (value - hi.astype(F32)).astype(BF16)


def dot(a, b):
    return jnp.dot(a, b, preferred_element_type=F32)


def pieces(total, size):
    return [(start, min(size, total - start)) for start in range(0, total, size)]


def window_of(chip, chips, ny):
    part = ny // chips
    width = part + LANE * min(chips - 1, 2)
    start = jnp.clip(chip * part - LANE, 0, ny - width)
    return pl.multiple_of(start, LANE), width


def body(
    nx, nz, ny, tiles, views,
    rec_ref, taps_ref, est_ref, out_ref,
    est_x, quo_x, rec_in, acc, acc_in, kern, mat_xz, mat_y, u_hi, u_lo,
    kern_send, kern_recv, rec_send, rec_recv, rim_send, rim_recv,
    acc_send, acc_recv, out_send, out_recv, fwd_send, fwd_recv,
):
    chips = views // CORES
    part = ny // chips
    rows = nx * nz
    rim = RADIUS * nz
    half = rows // 2
    tile = lax.axis_index("tile")
    view = lax.axis_index("view")
    chip, core = view // CORES, view % CORES
    mate = chip * CORES + (1 - core)
    start, width = window_of(chip, chips, ny)
    own = slice(rim, rim + rows)
    chunks = pieces(width, 2 * LANE)

    def chip_at(step):
        return lax.rem(chip + step, chips)

    def peer(step):
        return {"view": chip_at(step) * CORES + core}

    barrier = pltpu.get_barrier_semaphore()
    for step in range(1, chips):
        pl.semaphore_signal(barrier, inc=1, device_id=peer(step), device_id_type=MESH)
    pl.semaphore_signal(barrier, inc=1, device_id={"view": mate}, device_id_type=MESH)

    @pl.when(tile > 0)
    def _():
        pl.semaphore_signal(barrier, inc=1, device_id={"tile": tile - 1}, device_id_type=MESH)

    @pl.when(tile < tiles - 1)
    def _():
        pl.semaphore_signal(barrier, inc=1, device_id={"tile": tile + 1}, device_id_type=MESH)

    taps = taps_ref[:, 0, :]
    kern[0, 0:3, 0:TAPS] = taps / jnp.sum(taps, axis=1, keepdims=True)
    est_x[own, :] = est_ref[:, pl.ds(start, width)]

    @pl.when(tile == 0)
    def _():
        est_x[0:rim, :] = jnp.zeros((rim, width), F32)
        for s in range(chips):
            quo_x[s, 0:rim, :] = jnp.zeros((rim, width), F32)

    @pl.when(tile == tiles - 1)
    def _():
        est_x[rim + rows :, :] = jnp.zeros((rim, width), F32)
        for s in range(chips):
            quo_x[s, rim + rows :, :] = jnp.zeros((rim, width), F32)

    tile_peers = jnp.minimum(tile, 1) + jnp.minimum(tiles - 1 - tile, 1)
    pl.semaphore_wait(barrier, chips + tile_peers)

    def rim_copy(array, number, index, which):
        c0, n = chunks[index]
        near, far, neighbour = ((rim, rim + rows, tile - 1), (rows, 0, tile + 1))[which]
        return pltpu.make_async_remote_copy(
            src_ref=array.at[pl.ds(near, rim), pl.ds(c0, n)],
            dst_ref=array.at[pl.ds(far, rim), pl.ds(c0, n)],
            send_sem=rim_send.at[number, index, which],
            recv_sem=rim_recv.at[number, index, which],
            device_id={"tile": neighbour},
            device_id_type=MESH,
        )

    def rim_start(array, number, index):
        @pl.when(tile > 0)
        def _():
            rim_copy(array, number, index, 0).start()

        @pl.when(tile < tiles - 1)
        def _():
            rim_copy(array, number, index, 1).start()

    def rim_wait(array, number, index):
        @pl.when(tile > 0)
        def _():
            rim_copy(array, number, index, 0).wait_send()
            rim_copy(array, number, index, 1).wait_recv()

        @pl.when(tile < tiles - 1)
        def _():
            rim_copy(array, number, index, 1).wait_send()
            rim_copy(array, number, index, 0).wait_recv()

    for index in range(len(chunks)):
        rim_start(est_x, 0, index)

    def kern_copy(step):
        return pltpu.make_async_remote_copy(
            src_ref=kern.at[0],
            dst_ref=kern.at[step],
            send_sem=kern_send.at[step],
            recv_sem=kern_recv.at[step],
            device_id=peer(chips - step),
            device_id_type=MESH,
        )

    def rec_copy(step, index):
        c0, n = chunks[index]
        begin, _ = window_of(chip_at(chips - step), chips, ny)
        return pltpu.make_async_remote_copy(
            src_ref=rec_ref.at[:, pl.ds(pl.multiple_of(begin + c0, LANE), n)],
            dst_ref=rec_in.at[step, :, pl.ds(c0, n)],
            send_sem=rec_send.at[step, index],
            recv_sem=rec_recv.at[step, index],
            device_id=peer(chips - step),
            device_id_type=MESH,
        )

    for step in range(1, chips):
        kern_copy(step).start()
        rec_copy(step, 0).start()

    def build(s):
        kern_s = kern[s]
        width_s = mat_xz.shape[-1]
        wide = -(-width_s // LANE) * LANE
        a = lax.broadcasted_iota(jnp.int32, (nz, wide), 0)
        column = lax.broadcasted_iota(jnp.int32, (nz, wide), 1)
        p, b = lax.div(column, jnp.int32(nz)), lax.rem(column, jnp.int32(nz))
        r = lax.broadcasted_iota(jnp.int32, (3 * LANE, LANE), 0)
        c = lax.broadcasted_iota(jnp.int32, (3 * LANE, LANE), 1)
        for mirrored in range(2):
            fx = jnp.zeros((nz, wide), F32)
            fz = jnp.zeros((nz, wide), F32)
            fy = jnp.zeros((3 * LANE, LANE), F32)
            for k in range(TAPS):
                o = TAPS - 1 - k if mirrored else k
                fx = jnp.where(p == k, kern_s[0:1, o : o + 1], fx)
                fz = jnp.where(b - a + RADIUS == k, kern_s[1:2, o : o + 1], fz)
                fy = jnp.where(r - c - LANE + RADIUS == k, kern_s[2:3, o : o + 1], fy)
            strip = fx * fz
            for i in range(nx // 2):
                moved = strip if i == 0 else pltpu.roll(strip, i * nz, 1)
                hi, lo = split(moved)
                mat_xz[s, mirrored, i * nz : (i + 1) * nz, :] = hi[:, :width_s]
                mat_xz[s, mirrored, half + i * nz : half + (i + 1) * nz, :] = lo[:, :width_s]
            for index, value in enumerate(split(fy)):
                mat_y[s, mirrored, index, 0 : 3 * LANE, 0:LANE] = value
                mat_y[s, mirrored, index, LANE : 4 * LANE, LANE : 2 * LANE] = value
                mat_y[s, mirrored, index, 3 * LANE :, 0:LANE] = jnp.zeros((LANE, LANE), BF16)
                mat_y[s, mirrored, index, 0:LANE, LANE : 2 * LANE] = jnp.zeros((LANE, LANE), BF16)

    for u in (u_hi, u_lo):
        u[:, 0:LANE] = jnp.zeros((rows, LANE), BF16)
        u[:, LANE + width :] = jnp.zeros((rows, LANE), BF16)

    def blur(source, s, mirrored, ready, store, between=None):
        depth = half + 2 * rim

        def along_xz(index):
            c0, n = chunks[index]
            for h in range(2):
                hi, lo = split(source[h * half : h * half + depth, c0 : c0 + n])
                both = dot(mat_xz[s, mirrored], hi)
                value = both[:half] + both[half:] + dot(mat_xz[s, mirrored, :half], lo)
                hi, lo = split(value)
                u_hi[h * half : (h + 1) * half, LANE + c0 : LANE + c0 + n] = hi
                u_lo[h * half : (h + 1) * half, LANE + c0 : LANE + c0 + n] = lo

        def along_y(index):
            c0, n = chunks[index]
            k = n + 2 * LANE
            hi, lo = u_hi[:, c0 : c0 + k], u_lo[:, c0 : c0 + k]
            m_hi, m_lo = mat_y[s, mirrored, 0, :k, :n], mat_y[s, mirrored, 1, :k, :n]
            store(index, dot(hi, m_hi) + dot(lo, m_hi) + dot(hi, m_lo))

        for index in range(len(chunks)):
            ready(index)
            along_xz(index)
            if index > 0:
                along_y(index - 1)
            if index == 0 and between is not None:
                between()
        along_y(len(chunks) - 1)

    def swap(it, index):
        c0, n = chunks[index]
        return pltpu.make_async_remote_copy(
            src_ref=acc.at[:, pl.ds(c0, n)],
            dst_ref=acc_in.at[it, :, pl.ds(c0, n)],
            send_sem=acc_send.at[it, index],
            recv_sem=acc_recv.at[it, index],
            device_id={"view": mate},
            device_id_type=MESH,
        )

    def second_recorded():
        for step in range(1, chips):
            rec_copy(step, 0).wait_send()
            if len(chunks) > 1:
                rec_copy(step, 1).start()

    def later_recorded():
        for step in range(1, chips):
            for index in range(2, len(chunks)):
                rec_copy(step, index).start()

    def forward(it, s):
        quo = quo_x.at[s]

        def ready(index):
            if s == 0:
                rim_wait(est_x, 0, index)

        def store_quotient(index, blurred):
            c0, n = chunks[index]
            if s == 0:
                recorded = rec_ref[:, pl.ds(pl.multiple_of(start + c0, LANE), n)]
            else:
                if it == 0:
                    rec_copy(s, index).wait_recv()
                    if index > 0:
                        rec_copy(s, index).wait_send()
                recorded = rec_in[s, :, c0 : c0 + n]
            quo[own, c0 : c0 + n] = recorded / blurred
            rim_start(quo, 1 + s, index)

        first = it == 0 and s == 0
        blur(est_x, s, 0, ready, store_quotient, second_recorded if first else None)
        if first:
            later_recorded()

    def backward(it, s):
        quo = quo_x.at[s]

        def ready(index):
            rim_wait(quo, 1 + s, index)

        def store_log(index, value):
            c0, n = chunks[index]
            term = jnp.log(value)
            if s > 0:
                term = acc[:, c0 : c0 + n] + term
            acc[:, c0 : c0 + n] = term
            if s == chips - 1:
                swap(it, index).start()

        blur(quo, s, 1, ready, store_log)

    my_rows = pl.ds(pl.multiple_of(core * half, 8), half)
    inner = pl.multiple_of(chip * part - start, LANE)
    out_parts = pieces(part, 2 * LANE)

    def gather_copy(step, index, forwarded):
        c0, n = out_parts[index]
        owner = chip_at(chips - step) if forwarded else chip
        place = (my_rows, pl.ds(pl.multiple_of(owner * part + c0, LANE), n))
        send, recv = (fwd_send, fwd_recv) if forwarded else (out_send, out_recv)
        return pltpu.make_async_remote_copy(
            src_ref=out_ref.at[place],
            dst_ref=out_ref.at[place],
            send_sem=send.at[step, index],
            recv_sem=recv.at[step, index],
            device_id={"view": mate} if forwarded else peer(step),
            device_id_type=MESH,
        )

    def finish(index, which):
        c0, n = out_parts[index]
        there = pl.ds(pl.multiple_of(chip * part + c0, LANE), n)
        here = pl.ds(pl.multiple_of(inner + c0, LANE), n)
        begin = pl.multiple_of((core if which == 0 else 1 - core) * half, 8)
        row = pl.ds(begin, half)
        total = acc[row, here] + acc_in[ITERS - 1, row, here]
        out_ref[row, there] = est_x[pl.ds(pl.multiple_of(rim + begin, 8), half), here] * jnp.exp(
            total / views
        )

    build(0)
    for it in range(ITERS):
        for s in range(chips):
            if it == 0 and s > 0:
                kern_copy(s).wait()
                build(s)
            forward(it, s)
        for s in range(chips):
            backward(it, s)
        if it < ITERS - 1:
            for index, (c0, n) in enumerate(chunks):
                swap(it, index).wait()
                here = slice(c0, c0 + n)
                est_x[own, here] = est_x[own, here] * jnp.exp(
                    (acc[:, here] + acc_in[it, :, here]) / views
                )
                rim_start(est_x, 0, index)

    done = 0
    for index, (c0, n) in enumerate(out_parts):
        while done < len(chunks) and chunks[done][0] < width - part + c0 + n:
            swap(ITERS - 1, done).wait()
            done += 1
        finish(index, 0)
        for step in range(1, chips):
            gather_copy(step, index, False).start()
    for index in range(len(out_parts)):
        finish(index, 1)
    for index in range(len(out_parts)):
        for step in range(1, chips):
            gather_copy(step, index, False).wait_recv()
            gather_copy(step, index, True).start()
    for index in range(len(out_parts)):
        for step in range(1, chips):
            gather_copy(step, index, False).wait_send()
            gather_copy(step, index, True).wait()


def local(tiles, views, recorded, psf_taps, estimate):
    nx, nz, ny = estimate.shape
    rows, rim = nx * nz, RADIUS * nz
    chips = views // CORES
    width = window_of(0, chips, ny)[1]
    vmem = pl.BlockSpec(memory_space=pltpu.VMEM)
    dma = pltpu.SemaphoreType.DMA
    parts = len(pieces(width, 2 * LANE))
    outs = len(pieces(ny // chips, 2 * LANE))
    out = pl.pallas_call(
        functools.partial(body, nx, nz, ny, tiles, views),
        out_shape=jax.ShapeDtypeStruct((rows, ny), F32),
        in_specs=[vmem] * 3,
        out_specs=vmem,
        scratch_shapes=[
            pltpu.VMEM((rows + 2 * rim, width), F32),
            pltpu.VMEM((chips, rows + 2 * rim, width), F32),
            pltpu.VMEM((chips, rows, width), F32),
            pltpu.VMEM((rows, width), F32),
            pltpu.VMEM((ITERS, rows, width), F32),
            pltpu.VMEM((chips, 8, LANE), F32),
            pltpu.VMEM((chips, 2, rows, rows // 2 + 2 * rim), BF16),
            pltpu.VMEM((chips, 2, 2, 4 * LANE, 2 * LANE), BF16),
            pltpu.VMEM((rows, width + 2 * LANE), BF16),
            pltpu.VMEM((rows, width + 2 * LANE), BF16),
            dma((chips,)),
            dma((chips,)),
            dma((chips, parts)),
            dma((chips, parts)),
            dma((1 + chips, parts, 2)),
            dma((1 + chips, parts, 2)),
            dma((ITERS, parts)),
            dma((ITERS, parts)),
            dma((chips, outs)),
            dma((chips, outs)),
            dma((chips, outs)),
            dma((chips, outs)),
        ],
        compiler_params=pltpu.CompilerParams(
            collective_id=0, has_side_effects=True, vmem_limit_bytes=56 * 2**20
        ),
    )(recorded.reshape(rows, ny), psf_taps.reshape(3, 1, TAPS), estimate.reshape(rows, ny))
    return out.reshape(estimate.shape)


def solution(mesh):
    in_specs = (P("view", "tile", "slab", None), P("view", None, None), P("tile", "slab", None))
    out_specs = P("tile", "slab", None)
    sizes = (mesh.shape["tile"], mesh.shape["view"])
    return jax.shard_map(
        functools.partial(local, *sizes),
        mesh=mesh, in_specs=in_specs, out_specs=out_specs, check_vma=False,
    )
```

time: 81.2 us -> 76 us (0.936)
  Pallas kernels: 77.1 us -> 73.2 us
  local copies, waits for them, and re-layouts: 3.99 us -> 2.73 us
    pallas_call x1, Pallas kernels: 77.1 us -> 73.2 us  [local(): pl.pallas_call(functools.partial(body, nx, nz, ny, tiles, views), out_sha...]
    unnamed x2 -> x1, local copies, waits for them, and re-layouts: 3.99 us -> 2.73 us
where the time goes in v2:
time: 76 us; the launch traced here: 75.9 us
  Pallas kernels  73.2 us (96%)
  local copies, waits for them, and re-layouts  2.73 us (4%)
    pallas_call x1, Pallas kernels, local(): pl.pallas_call(functools.partial(body, nx, nz, ny, tiles, views), out_sha...  73.2 us
    unnamed x1, local copies, waits for them, and re-layouts  2.73 us

profile of v2, /device:TPU:0, one launch (start us, length us, event | category | flops | bytes accessed | tf_op | source)
XLA Modules:
  0.0 75.9 jit_solution(5813127984743863473)
XLA Ops:
  0.0 73.2 %shard_map.37 = f32[384,1024]{1,0:T(8,128)} custom-call(f32[384,1024]{1,0:T(8,128)} %bitcast.5, f32[3,1,15]{2,1,0:T(1,128)} %bitcast.7, f32[384,1024]{1,0:T(8,128)} %bitcast.6), custom_call_target="tpu_custom_call" | custom-call | tf_op jit(solution)/shard_map/pallas_call | solution.py:362
  73.2 2.7 %copy.5 = f32[24,16,1024]{2,1,0:T(8,128)} copy(f32[24,16,1024]{2,1,0:T(8,128)} %bitcast.4) | data formatting | bytes 3145728
